TPU v7x, 512 devices: a whole 4x4x16 slice. The times are simulated.
512 devices in a mesh: pi: 16 (over x, z_hi, core), pj: 32 (over z_lo, y).
Axes of the slice: x: 4, y: 4, z: 16 (z_hi: 2, z_lo: 8; z = z_hi * 8 + z_lo), core: 2. Of those that a mesh axis runs over, the one named last changes fastest.
Arguments:
- amplitudes: bfloat16 [32, 32, 128, 128], P('pi', 'pj'), may hold values from -6 to 6
- cholesky: bfloat16 [128, 128, 4096], P(None, None, 'pj'), may hold values from -1 to 1, as said below
- other_terms: float32 [32, 32, 128, 128], P('pi', 'pj'), may hold values from -6 to 6
Outputs:
- residual: float32 [32, 32, 128, 128], P('pi', 'pj')
Inputs may be any that keep to these rules, and one draw needn't show every extreme that they name: cholesky[x, y, P] equals cholesky[y, x, P].
All inputs are finite; a program needn't handle non-finite values.
Results may differ from a plain program's by a relative error of at most 0.0036.
Values may be sent and summed in bfloat16 or wider, within the bound.
A program may use at most 64 MiB of HBM per device.

v0:
```python
import jax
import jax.numpy as jnp
from jax import lax
from jax.sharding import PartitionSpec as P


def from_partner(block, axis, apart):
    count = lax.axis_size(axis)
    route = []
    for low in range(count):
        high = low | 1 << apart
        if high != low and high < count:
            route += [(low, high), (high, low)]
    return lax.ppermute(block, axis, route)


def product(left, right):
    return jnp.einsum("cap,bdp->abcd", left, right, preferred_element_type=jnp.float32)


def ladder_rows(source, flat, tile_shape, count):
    inner = source.shape[1]
    matrix = source.reshape(count * inner, -1)
    result = lax.dot_general(
        matrix, flat, (((1,), (1,)), ((), ())), preferred_element_type=jnp.float32
    )
    return result.reshape(count, inner, tile_shape[0], tile_shape[1])


def shards(amplitudes, cholesky, other_terms):
    width = cholesky.shape[0]
    pair_i = amplitudes.shape[0]
    pair_j = amplitudes.shape[1]
    count_i = lax.axis_size("pi")
    block_i = width // count_i
    row_index = lax.axis_index("pi")
    col_index = lax.axis_index("pj")
    from_j = lax.all_to_all(cholesky, "pj", split_axis=0, concat_axis=2, tiled=True)
    own_rows = lax.dynamic_slice_in_dim(cholesky, row_index * block_i, block_i, 0)
    from_i = lax.all_gather(own_rows, "pj", axis=2, tiled=True)
    total = product(from_i, from_j)
    tile = total.astype(jnp.bfloat16)
    tile_shape = (tile.shape[0], tile.shape[1])
    flat = tile.reshape(tile.shape[0] * tile.shape[1], tile.shape[2] * tile.shape[3])
    split = lax.all_to_all(amplitudes, "pi", split_axis=2, concat_axis=0, tiled=True)
    gathered = lax.all_gather(split, "pj", axis=1, tiled=True)
    sums = lax.psum_scatter(
        ladder_rows(gathered, flat, tile_shape, lax.axis_size("pi") * pair_i),
        "pi",
        scatter_dimension=0,
        tiled=True,
    )
    ladder = lax.all_to_all(sums, "pj", split_axis=1, concat_axis=3, tiled=True)
    half = (other_terms + 0.5 * ladder).astype(jnp.bfloat16)
    halves = half.reshape(2, pair_j, pair_j, width, width)
    parity = col_index % 2
    retained = jnp.where(parity == 0, halves[0], halves[1])
    outgoing = jnp.where(parity == 0, halves[1], halves[0])
    received = from_partner(outgoing, "pj", 0)
    buffer = jnp.where(
        parity == 0, jnp.stack([retained, received]), jnp.stack([received, retained])
    )
    upper = col_index // 2
    levels = count_i.bit_length() - 1
    for level in range(levels):
        across = from_partner(buffer, "pi", level)
        across = from_partner(across, "pj", level + 1)
        differ = row_index // 2**level % 2 != upper // 2**level % 2
        buffer = jnp.where(differ, across, buffer)
    mirrored = jnp.transpose(buffer, (0, 2, 1, 4, 3)).reshape(pair_i, pair_j, width, width)
    return half.astype(jnp.float32) + mirrored.astype(jnp.float32)


def solution(mesh):
    return jax.shard_map(
        shards,
        mesh=mesh,
        in_specs=(P("pi", "pj", None, None), P(None, None, "pj"), P("pi", "pj", None, None)),
        out_specs=P("pi", "pj", None, None),
        check_vma=False,
    )
```

profile of v0, /device:TPU:7, one launch (start us, length us, event | category | flops | bytes accessed | tf_op | source)
XLA Modules:
  0.0 728.1 jit_solution(3555316031862831923)
XLA Ops:
  6.5 0.0 all-gather.5.cloned.1.call-start
  6.5 0.9 copy.27
  7.4 31.0 %all_to_all.45 = bf16[2,1,128,128]{3,0,1,2:T(2,128)(2,1)S(1)} all-to-all(bf16[2,1,128,128]{3,0,1,2:T(2,128)(2,1)S(1)} %copy.27), channel_id=1, replica_groups=mesh['pi'=16,'pj'=32] {'pi'}, dimensions={2} | all-to-all | bytes 131072 | tf_op jit(solution)/shard_map/all_to_all | solution.py:45
  38.4 0.6 copy.29
  39.1 0.0 all-gather.5.cloned.1.call-update
  39.1 7.9 %all-to-all-start = ((bf16[128,128,128]{2,1,0:T(8,128)(2,1)}), bf16[128,128,128]{2,1,0:T(8,128)(2,1)}, u32[]{:S(2)}, u32[]{:S(2)}) async-start(bf16[128,128,128]{2,1,0:T(8,128)(2,1)} %param.4), calls=%async_computation | async-start | bytes 8388608 | tf_op jit(solution)/shard_map/all_to_all | solution.py:38
  47.0 0.0 all-gather.3.cloned.1.call-start
  47.1 1.7 constant_dynamic-slice_fusion
  48.7 0.0 all-gather.3.cloned.1.call-update
  48.8 0.0 reduce-scatter.2.cloned.1.call-start
  48.8 196.9 %all-gather.5.cloned.1.call-done = bf16[32,32,8,128]{3,2,0,1:T(8,128)(2,1)} async-done(((bf16[32,1,8,128]{3,2,0,1:T(8,128)(2,1)}), bf16[32,32,8,128]{3,2,0,1:T(8,128)(2,1)}) %all-gather.5.cloned.1.call-update) | async-done | bytes 2097168 | tf_op jit(solution)/shard_map/all_gather | solution.py:46
  245.7 3.5 copy.30
  249.2 1.9 all-to-all-done
  251.2 6.8 copy.56
  258.0 7.3 %reshape.118 = bf16[4,128,4096,1]{2,1,0,3:T(8,128)(2,1)} reshape(bf16[4,128,32,128]{3,2,1,0:T(8,128)(2,1)} %bitcast.64) | data formatting | bytes 8388608 | tf_op jit(solution)/shard_map/all_to_all | solution.py:38
  265.3 213.7 %all-gather.3.cloned.1.call-done = bf16[8,128,4096]{2,1,0:T(8,128)(2,1)} async-done(((bf16[8,128,128]{2,1,0:T(8,128)(2,1)}), bf16[8,128,4096]{2,1,0:T(8,128)(2,1)}) %all-gather.3.cloned.1.call-update) | async-done | bytes 8388624 | tf_op jit(solution)/shard_map/all_gather | solution.py:40
  479.0 8.4 %fusion.11 = bf16[128,4,8,128]{3,0,1,2:T(8,128)(2,1)S(1)} fusion(bf16[4,128,4096,1]{2,1,0,3:T(8,128)(2,1)} %reshape.118, bf16[8,128,4096]{2,1,0:T(8,128)(2,1)} %all-gather.3.cloned.1.call-done), kind=kOutput, calls=%fused_computation.8 | convolution fusion | flops 4295491584 | bytes 13631488 | tf_op jit(solution)/shard_map/cap,bdp->abcd/dot_general | solution.py:18
  487.4 0.7 copy.26
  488.1 1.3 fusion.5
  489.4 4.8 reshape.115
  494.2 7.6 %copy.31 = f32[32,32,128,4]{2,1,3,0:T(8,128)} copy(f32[32,32,128,4]{1,0,3,2:T(8,128)} %reshape.115) | data formatting | bytes 4194304 | tf_op jit(solution)/shard_map/reshape | solution.py:27
  501.8 0.0 reduce-scatter.2.cloned.1.call-update
  501.8 131.1 %reduce-scatter.2.cloned.1.call-done = f32[2,32,128,4]{2,1,3,0:T(8,128)} async-done(((f32[32,32,128,4]{2,1,3,0:T(8,128)}), f32[2,32,128,4]{2,1,3,0:T(8,128)}) %reduce-scatter.2.cloned.1.call-update) | async-done | bytes 131088 | tf_op jit(solution)/shard_map/reduce_scatter | solution.py:47
  632.9 1.6 copy.32
  634.5 4.7 all-to-all-start.2
  639.2 0.0 copy-done.1
  639.2 0.1 copy.34
  639.4 12.0 %all-to-all-done.2 = f32[2,32,128,4]{2,3,0,1:T(4,128)S(1)} async-done(((f32[2,32,128,4]{2,3,0,1:T(4,128)}), f32[2,32,128,4]{2,3,0,1:T(4,128)S(1)}, u32[]{:S(2)}, u32[]{:S(2)}) %all-to-all-start.2) | async-done | bytes 131104 | tf_op jit(solution)/shard_map/all_to_all | solution.py:53
  651.4 2.2 collective-permute-start
  653.7 2.4 collective-permute-done
  656.1 6.8 collective-permute-start.1
  662.9 0.9 collective-permute-done.1
  663.8 3.2 collective-permute-start.2
  667.1 3.2 collective-permute-done.2
  670.3 7.8 %collective-permute-start.3 = (bf16[2,1,1,128,128]{3,4,2,1,0:T(8,128)(2,1)S(1)}, bf16[2,1,1,128,128]{3,4,2,1,0:T(8,128)(2,1)S(1)}, u32[]{:S(2)}, u32[]{:S(2)}) collective-permute-start(bf16[2,1,1,128,128]{3,4,2,1,0:T(8,128)(2,1)S(1)} %broadcast_select_fusion), channel_id=1, source_target_pairs={{0,64},{64,0},{32,96},{96,32},{128,192},{192,128},{160,224},{224,1... | collective-permute-start | bytes 196616 | tf_op jit(solution)/shard_map/ppermute | solution.py:14
  678.1 6.4 collective-permute-done.3
  684.5 6.5 collective-permute-start.4
  691.1 1.6 collective-permute-done.4
  692.6 1.9 collective-permute-start.5
  694.6 3.1 collective-permute-done.5
  697.7 1.9 collective-permute-start.6
  699.6 3.9 collective-permute-done.6
  703.6 3.0 collective-permute-start.7
  706.5 3.5 collective-permute-done.7
  710.1 1.9 collective-permute-start.8
  712.1 0.1 copy.35
  712.2 8.7 %collective-permute-done.8 = bf16[2,1,1,128,128]{3,4,2,1,0:T(8,128)(2,1)S(1)} collective-permute-done((bf16[2,1,1,128,128]{3,4,2,1,0:T(8,128)(2,1)S(1)}, bf16[2,1,1,128,128]{3,4,2,1,0:T(8,128)(2,1)S(1)}, u32[]{:S(2)}, u32[]{:S(2)}) %collective-permute-start.8) | collective-permute-done | bytes 65568 | tf_op jit(solution)/shard_map/ppermute | solution.py:14
  720.9 0.7 fusion.16
  (13 shorter events, 0.2 us)
Async XLA Ops:
  6.5 239.2 %all-gather.5.cloned.1.call-start = ((), (), s32[]{:S(2)}) async-start(), calls=%async_computation.5 | async-start | bytes 2162688 | tf_op jit(solution)/shard_map/all_gather | solution.py:46
  39.1 212.1 %all-to-all-start = ((bf16[128,128,128]{2,1,0:T(8,128)(2,1)}), bf16[128,128,128]{2,1,0:T(8,128)(2,1)}, u32[]{:S(2)}, u32[]{:S(2)}) async-start(bf16[128,128,128]{2,1,0:T(8,128)(2,1)} %param.4), calls=%async_computation | async-start | bytes 8388608 | tf_op jit(solution)/shard_map/all_to_all | solution.py:38
  47.0 432.0 %all-gather.3.cloned.1.call-start = ((), (), s32[]{:S(2)}) async-start(), calls=%async_computation.4 | async-start | bytes 8650752 | tf_op jit(solution)/shard_map/all_gather | solution.py:40
  48.8 584.1 %reduce-scatter.2.cloned.1.call-start = ((), (), s32[]{:S(2)}) async-start(), calls=%async_computation.6 | async-start | bytes 2228224 | tf_op jit(solution)/shard_map/reduce_scatter | solution.py:47
  479.0 9.1 %copy-start = (bf16[32,32,8,128]{3,2,1,0:T(8,128)(2,1)S(1)}, bf16[32,32,8,128]{3,2,1,0:T(8,128)(2,1)}, u32[]{:S(2)}) copy-start(bf16[32,32,8,128]{3,2,1,0:T(8,128)(2,1)} %copy.30) | copy-start | bytes 6291460
  494.2 145.1 %copy-start.1 = (f32[2,1,128,128]{3,2,1,0:T(8,128)S(1)}, f32[2,1,128,128]{3,2,1,0:T(8,128)}, u32[]{:S(2)}) copy-start(f32[2,1,128,128]{3,2,1,0:T(8,128)} %param.5) | copy-start | bytes 393220
  634.5 16.8 %all-to-all-start.2 = ((f32[2,32,128,4]{2,3,0,1:T(4,128)}), f32[2,32,128,4]{2,3,0,1:T(4,128)S(1)}, u32[]{:S(2)}, u32[]{:S(2)}) async-start(f32[2,32,128,4]{2,3,0,1:T(4,128)} %copy.32), calls=%async_computation.3 | async-start | bytes 262144 | tf_op jit(solution)/shard_map/all_to_all | solution.py:53
  651.4 4.7 collective-permute-start
  656.1 7.6 %collective-permute-start.1 = (bf16[2,1,1,128,128]{3,4,2,1,0:T(8,128)(2,1)S(1)}, bf16[2,1,1,128,128]{3,4,2,1,0:T(8,128)(2,1)S(1)}, u32[]{:S(2)}, u32[]{:S(2)}) collective-permute-start(bf16[2,1,1,128,128]{3,4,2,1,0:T(8,128)(2,1)S(1)} %maximum_select_fusion), channel_id=1, source_target_pairs={{0,32},{32,0},{64,96},{96,64},{128,160},{160,128},{192,224},{224,1... | collective-permute-start | bytes 196616 | tf_op jit(solution)/shard_map/ppermute | solution.py:14
  663.8 6.5 collective-permute-start.2
  670.3 14.2 %collective-permute-start.3 = (bf16[2,1,1,128,128]{3,4,2,1,0:T(8,128)(2,1)S(1)}, bf16[2,1,1,128,128]{3,4,2,1,0:T(8,128)(2,1)S(1)}, u32[]{:S(2)}, u32[]{:S(2)}) collective-permute-start(bf16[2,1,1,128,128]{3,4,2,1,0:T(8,128)(2,1)S(1)} %broadcast_select_fusion), channel_id=1, source_target_pairs={{0,64},{64,0},{32,96},{96,32},{128,192},{192,128},{160,224},{224,1... | collective-permute-start | bytes 196616 | tf_op jit(solution)/shard_map/ppermute | solution.py:14
  684.5 8.2 %collective-permute-start.4 = (bf16[2,1,1,128,128]{3,4,2,1,0:T(8,128)(2,1)S(1)}, bf16[2,1,1,128,128]{3,4,2,1,0:T(8,128)(2,1)S(1)}, u32[]{:S(2)}, u32[]{:S(2)}) collective-permute-start(bf16[2,1,1,128,128]{3,4,2,1,0:T(8,128)(2,1)S(1)} %collective-permute-done.3), channel_id=1, source_target_pairs={{0,4},{4,0},{1,5},{5,1},{2,6},{6,2},{3,7},{7,3},{8,12},{12,8},{9,1... | collective-permute-start | bytes 196616 | tf_op jit(solution)/shard_map/ppermute | solution.py:14
  692.6 5.0 collective-permute-start.5
  697.7 5.9 collective-permute-start.6
  703.6 6.5 collective-permute-start.7
  710.1 10.8 %collective-permute-start.8 = (bf16[2,1,1,128,128]{3,4,2,1,0:T(8,128)(2,1)S(1)}, bf16[2,1,1,128,128]{3,4,2,1,0:T(8,128)(2,1)S(1)}, u32[]{:S(2)}, u32[]{:S(2)}) collective-permute-start(bf16[2,1,1,128,128]{3,4,2,1,0:T(8,128)(2,1)S(1)} %collective-permute-done.7), channel_id=1, source_target_pairs={{0,16},{16,0},{1,17},{17,1},{2,18},{18,2},{3,19},{19,3},{4,20},{20... | collective-permute-start | bytes 196616 | tf_op jit(solution)/shard_map/ppermute | solution.py:14
Sparse Core Ops, SparseCore 0:
  39.2 206.4 all-gather.4
  247.7 231.2 all-gather.2
  501.9 130.9 reduce-scatter.1
where the time goes:
time: 735 us; the launch traced here: 728 us
  waiting for transfers between devices  589 us (80%)
  starting transfers between devices  47.9 us (7%)
  local copies, waits for them, and re-layouts  35.8 us (5%)
  blocking collectives  31 us (4%)
  between operations  13.6 us (2%)
  matrix products  9.64 us (1%)
    all_gather x1, waiting for transfers between devices, shards(): from_i = lax.all_gather(own_rows, 'pj', axis=2, tiled=True)  214 us
    all_gather x1, waiting for transfers between devices, shards(): gathered = lax.all_gather(split, 'pj', axis=1, tiled=True)  197 us
    reduce_scatter x1, waiting for transfers between devices, shards(): lax.psum_scatter(ladder_rows(gathered, flat, tile_shape, lax.axis_size('p...  131 us
    ppermute x9, starting transfers between devices, from_partner(): return lax.ppermute(block, axis, route)  35.2 us
    ppermute x9, waiting for transfers between devices, from_partner(): return lax.ppermute(block, axis, route)  33.7 us
    all_to_all x1, blocking collectives, shards(): lax.all_to_all(amplitudes, 'pi', split_axis=2, concat_axis=0, tiled=True)  31 us
  transfers between devices with their start and end apart: 14, of which 14 were waited for; matrix products, arithmetic and copies ran while one was open for 3% of the time, Pallas kernels for 0%

commit v1 on v0

v1 whole, which is shorter than its diff:
```python
import jax
import jax.numpy as jnp
from jax import lax
from jax.sharding import PartitionSpec as P


def spread(block, axis):
    count = lax.axis_size(axis)
    copies = jnp.broadcast_to(block[None], (count,) + block.shape)
    return lax.all_to_all(copies, axis, split_axis=0, concat_axis=0, tiled=True)


def mirror_route(count_i, count_j, turn):
    route = []
    for row in range(count_i):
        for col in range(count_j):
            target = (col // 2) * count_j + 2 * row + (turn + col) % 2
            route.append((row * count_j + col, target))
    return route


def shards(amplitudes, cholesky, other_terms):
    width = cholesky.shape[0]
    pair_i = amplitudes.shape[0]
    count_i = lax.axis_size("pi")
    count_j = lax.axis_size("pj")
    depth = cholesky.shape[2]
    block_i = width // count_i
    block_j = width // count_j
    row_index = lax.axis_index("pi")
    col_index = lax.axis_index("pj")
    split = lax.all_to_all(
        amplitudes[:, 0], "pi", split_axis=1, concat_axis=0, tiled=True
    )
    gathered = spread(split, "pj")
    own_rows = lax.dynamic_slice_in_dim(cholesky, row_index * block_i, block_i, 0)
    from_i = spread(own_rows, "pj")
    from_j = lax.all_to_all(
        cholesky.reshape(count_j, block_j, width, depth), "pj", 0, 0, tiled=True
    )
    total = jnp.einsum("kcap,kbdp->cdba", from_i, from_j, preferred_element_type=jnp.float32)
    tile = total.astype(jnp.bfloat16)
    sums = jnp.einsum("jicd,cdba->ijba", gathered, tile, preferred_element_type=jnp.float32)
    parts = lax.all_to_all(
        sums.reshape(count_i, pair_i, count_j, block_j, width), "pi", 0, 0, tiled=True
    )
    summed = jnp.sum(parts, axis=0)
    ladder = lax.all_to_all(summed, "pj", split_axis=1, concat_axis=1, tiled=True)
    ladder = ladder.reshape(pair_i, width, width).swapaxes(1, 2)
    half = (other_terms[:, 0] + 0.5 * ladder).astype(jnp.bfloat16)
    odd = col_index % 2 == 1
    received = []
    for turn in range(2):
        outgoing = jnp.where(odd, half[1 - turn], half[turn])
        received.append(
            lax.ppermute(outgoing, ("pi", "pj"), mirror_route(count_i, count_j, turn))
        )
    first = jnp.where(odd, received[1], received[0])
    second = jnp.where(odd, received[0], received[1])
    mirrored = jnp.stack([first, second]).swapaxes(1, 2)
    return (half.astype(jnp.float32) + mirrored.astype(jnp.float32))[:, None]


def solution(mesh):
    return jax.shard_map(
        shards,
        mesh=mesh,
        in_specs=(P("pi", "pj", None, None), P(None, None, "pj"), P("pi", "pj", None, None)),
        out_specs=P("pi", "pj", None, None),
        check_vma=False,
    )
```

time: 735 us -> 868 us (1.18)
  waiting for transfers between devices: 589 us -> 666 us
  blocking collectives: 31 us -> 107 us
  local copies, waits for them, and re-layouts: 35.8 us -> 11.4 us
  starting transfers between devices: 47.9 us -> 72.2 us
  between operations: 13.6 us -> 0.17 us
    all_to_all x2 -> x4, waiting for transfers between devices: 13.9 us -> 657 us  [the longest x2 458 us: spread(): return lax.all_to_all(copies, axis, split_axis=0, concat_axis=0, tiled=True)]
    all_gather x2 -> x0, waiting for transfers between devices: 411 us -> none  [the longest x1 214 us: shards(): from_i = lax.all_gather(own_rows, 'pj', axis=2, tiled=True)]
    reduce_scatter x1 -> x0, waiting for transfers between devices: 131 us -> none  [shards(): lax.psum_scatter(ladder_rows(gathered, flat, tile_shape, lax.axis_size('p...]
    all_to_all x1 -> x2, blocking collectives: 31 us -> 107 us  [the longest x1 75.9 us: shards(): lax.all_to_all(sums.reshape(count_i, pair_i, count_j, block_j, width), 'p...]
    all_to_all x2 -> x4, starting transfers between devices: 12.6 us -> 57.4 us  [the longest x1 34.3 us: shards(): lax.all_to_all(summed, 'pj', split_axis=1, concat_axis=1, tiled=True)]
    ppermute x9 -> x2, waiting for transfers between devices: 33.7 us -> 8.97 us  [shards(): lax.ppermute(outgoing, ('pi', 'pj'), mirror_route(count_i, count_j, turn))]
    ppermute x9 -> x2, starting transfers between devices: 35.2 us -> 14.8 us  [shards(): lax.ppermute(outgoing, ('pi', 'pj'), mirror_route(count_i, count_j, turn))]
    all_to_all x4 -> x1, local copies, waits for them, and re-layouts: 14.8 us -> 0.05 us  [shards(): lax.all_to_all(amplitudes[:, 0], 'pi', split_axis=1, concat_axis=0, tiled...]
  transfers between devices with their start and end apart: 14 -> 6, of which waited for: 14 -> 6; matrix products, arithmetic and copies ran while one was open for 3% -> 1% of each run, Pallas kernels for 0% -> 0%
where the time goes in v1:
time: 868 us
  waiting for transfers between devices  666 us (77%)
  blocking collectives  107 us (12%)
  starting transfers between devices  72.2 us (8%)
  local copies, waits for them, and re-layouts  11.4 us (1%)
  matrix products  9.53 us (1%)
    all_to_all x2, waiting for transfers between devices, spread(): return lax.all_to_all(copies, axis, split_axis=0, concat_axis=0, tiled=True)  458 us
    all_to_all x1, waiting for transfers between devices, shards(): lax.all_to_all(cholesky.reshape(count_j, block_j, width, depth), 'pj', 0,...  187 us
    all_to_all x1, blocking collectives, shards(): lax.all_to_all(sums.reshape(count_i, pair_i, count_j, block_j, width), 'p...  75.9 us
    all_to_all x1, starting transfers between devices, shards(): lax.all_to_all(summed, 'pj', split_axis=1, concat_axis=1, tiled=True)  34.3 us
    all_to_all x1, blocking collectives, shards(): lax.all_to_all(amplitudes[:, 0], 'pi', split_axis=1, concat_axis=0, tiled...  31 us
  transfers between devices with their start and end apart: 6, of which 6 were waited for; matrix products, arithmetic and copies ran while one was open for 1% of the time, Pallas kernels for 0%

profile of v1, /device:TPU:7, one launch (start us, length us, event | category | flops | bytes accessed | tf_op | source)
XLA Modules:
  0.0 867.6 jit_solution(7771678990863366945)
XLA Ops:
  0.0 0.9 copy.85
  0.9 31.0 %all_to_all.40 = bf16[2,128,128]{2,0,1:T(2,128)(2,1)S(1)} all-to-all(bf16[2,128,128]{2,0,1:T(2,128)(2,1)S(1)} %bitcast.68), channel_id=1, replica_groups=mesh['pi'=16,'pj'=32] {'pi'}, dimensions={1} | all-to-all | bytes 131072 | tf_op jit(solution)/shard_map/all_to_all | solution.py:32
  31.9 7.9 all-to-all-start.1
  39.8 1.0 constant_dynamic-slice_fusion
  40.8 186.7 %all-to-all-done.1 = bf16[32,4,128,128]{3,2,1,0:T(8,128)(2,1)} async-done(((bf16[32,4,128,128]{3,2,1,0:T(8,128)(2,1)}), bf16[32,4,128,128]{3,2,1,0:T(8,128)(2,1)}, u32[]{:S(2)}, u32[]{:S(2)}) %all-to-all-start.1) | async-done | bytes 4194336 | tf_op jit(solution)/shard_map/all_to_all | solution.py:38
  227.4 5.4 broadcast_in_dim.8
  232.8 6.3 all-to-all-start
  239.2 371.8 %all-to-all-done = bf16[32,8,128,128]{3,2,1,0:T(8,128)(2,1)} async-done(((bf16[32,8,128,128]{3,2,1,0:T(8,128)(2,1)}), bf16[32,8,128,128]{3,2,1,0:T(8,128)(2,1)}, u32[]{:S(2)}, u32[]{:S(2)}) %all-to-all-start) | async-done | bytes 8388640 | tf_op jit(solution)/shard_map/all_to_all | solution.py:10
  611.0 1.8 broadcast_in_dim.19
  612.8 8.8 %all-to-all-start.3 = ((bf16[32,32,8,128]{3,1,2,0:T(8,128)(2,1)}), bf16[32,32,8,128]{3,1,2,0:T(8,128)(2,1)S(1)}, u32[]{:S(2)}, u32[]{:S(2)}) async-start(bf16[32,32,8,128]{3,1,2,0:T(8,128)(2,1)} %broadcast_in_dim.19), calls=%async_computation.3 | async-start | bytes 4194304 | tf_op jit(solution)/shard_map/all_to_all | solution.py:10
  621.7 8.2 fusion.10
  630.0 86.3 %all-to-all-done.3 = bf16[32,32,8,128]{3,1,2,0:T(8,128)(2,1)S(1)} async-done(((bf16[32,32,8,128]{3,1,2,0:T(8,128)(2,1)}), bf16[32,32,8,128]{3,1,2,0:T(8,128)(2,1)S(1)}, u32[]{:S(2)}, u32[]{:S(2)}) %all-to-all-start.3) | async-done | bytes 2097184 | tf_op jit(solution)/shard_map/all_to_all | solution.py:10
  716.3 1.3 fusion.4
  717.6 1.2 copy.53
  718.7 0.0 copy-start
  718.8 75.9 %all_to_all.41 = f32[16,2,32,4,128]{4,1,2,3,0:T(2,128)S(1)} all-to-all(f32[16,2,32,4,128]{4,1,2,3,0:T(2,128)S(1)} %copy.53), channel_id=1, replica_groups=mesh['pi'=16,'pj'=32] {'pi'}, dimensions={0} | all-to-all | bytes 4194304 | tf_op jit(solution)/shard_map/all_to_all | solution.py:44
  794.6 1.0 reduce_sum.9
  795.6 0.7 copy.55
  796.3 34.3 %all-to-all-start.5 = ((f32[2,32,4,128]{3,2,0,1:T(4,128)}), f32[2,32,4,128]{3,2,0,1:T(4,128)S(1)}, u32[]{:S(2)}, u32[]{:S(2)}) async-start(f32[2,32,4,128]{3,2,0,1:T(4,128)} %copy.55), calls=%async_computation.5 | async-start | bytes 262144 | tf_op jit(solution)/shard_map/all_to_all | solution.py:48
  830.7 0.0 copy-done
  830.7 0.1 copy.47
  830.8 12.0 %all-to-all-done.5 = f32[2,32,4,128]{3,2,0,1:T(4,128)S(1)} async-done(((f32[2,32,4,128]{3,2,0,1:T(4,128)}), f32[2,32,4,128]{3,2,0,1:T(4,128)S(1)}, u32[]{:S(2)}, u32[]{:S(2)}) %all-to-all-start.5) | async-done | bytes 131104 | tf_op jit(solution)/shard_map/all_to_all | solution.py:48
  842.8 0.1 copy.57
  843.0 8.5 collective-permute-start
  851.5 6.4 collective-permute-start.1
  857.8 0.1 copy.58
  858.0 0.3 collective-permute-done
  858.3 8.7 collective-permute-done.1
  866.9 0.7 fusion.15
  (5 shorter events, 0.1 us)
Async XLA Ops:
  31.9 195.5 %all-to-all-start.1 = ((bf16[32,4,128,128]{3,2,1,0:T(8,128)(2,1)}), bf16[32,4,128,128]{3,2,1,0:T(8,128)(2,1)}, u32[]{:S(2)}, u32[]{:S(2)}) async-start(bf16[32,4,128,128]{3,2,1,0:T(8,128)(2,1)} %bitcast.63), calls=%async_computation.1 | async-start | bytes 8388608 | tf_op jit(solution)/shard_map/all_to_all | solution.py:38
  232.8 378.2 %all-to-all-start = ((bf16[32,8,128,128]{3,2,1,0:T(8,128)(2,1)}), bf16[32,8,128,128]{3,2,1,0:T(8,128)(2,1)}, u32[]{:S(2)}, u32[]{:S(2)}) async-start(bf16[32,8,128,128]{3,2,1,0:T(8,128)(2,1)} %broadcast_in_dim.8), calls=%async_computation | async-start | bytes 16777216 | tf_op jit(solution)/shard_map/all_to_all | solution.py:10
  612.8 103.4 %all-to-all-start.3 = ((bf16[32,32,8,128]{3,1,2,0:T(8,128)(2,1)}), bf16[32,32,8,128]{3,1,2,0:T(8,128)(2,1)S(1)}, u32[]{:S(2)}, u32[]{:S(2)}) async-start(bf16[32,32,8,128]{3,1,2,0:T(8,128)(2,1)} %broadcast_in_dim.19), calls=%async_computation.3 | async-start | bytes 4194304 | tf_op jit(solution)/shard_map/all_to_all | solution.py:10
  718.7 111.9 %copy-start = (f32[2,1,128,128]{3,2,1,0:T(8,128)S(1)}, f32[2,1,128,128]{3,2,1,0:T(8,128)}, u32[]{:S(2)}) copy-start(f32[2,1,128,128]{3,2,1,0:T(8,128)} %param.5) | copy-start | bytes 393220
  796.3 46.5 %all-to-all-start.5 = ((f32[2,32,4,128]{3,2,0,1:T(4,128)}), f32[2,32,4,128]{3,2,0,1:T(4,128)S(1)}, u32[]{:S(2)}, u32[]{:S(2)}) async-start(f32[2,32,4,128]{3,2,0,1:T(4,128)} %copy.55), calls=%async_computation.5 | async-start | bytes 262144 | tf_op jit(solution)/shard_map/all_to_all | solution.py:48
  843.0 15.3 %collective-permute-start = (bf16[128,128]{0,1:T(8,128)(2,1)S(1)}, bf16[128,128]{0,1:T(8,128)(2,1)S(1)}, u32[]{:S(2)}, u32[]{:S(2)}) collective-permute-start(bf16[128,128]{0,1:T(8,128)(2,1)S(1)} %get-tuple-element.7), channel_id=1, source_target_pairs={{0,1},{1,0},{2,33},{3,32},{4,65},{5,64},{6,97},{7,96},{8,129},{9,1... | collective-permute-start | bytes 98312 | tf_op jit(solution)/shard_map/ppermute | solution.py:56
  851.5 15.5 %collective-permute-start.1 = (bf16[128,128]{0,1:T(8,128)(2,1)S(1)}, bf16[128,128]{0,1:T(8,128)(2,1)S(1)}, u32[]{:S(2)}, u32[]{:S(2)}) collective-permute-start(bf16[128,128]{0,1:T(8,128)(2,1)S(1)} %get-tuple-element.8), channel_id=1, source_target_pairs={{0,0},{1,1},{2,32},{3,33},{4,64},{5,65},{6,96},{7,97},{8,128},{9,1... | collective-permute-start | bytes 98312 | tf_op jit(solution)/shard_map/ppermute | solution.py:56

commit v2 on v1

v2 whole, which is shorter than its diff:
```python
import jax
import jax.numpy as jnp
from jax import lax
from jax.experimental import pallas as pl
from jax.experimental.pallas import tpu as pltpu
from jax.sharding import PartitionSpec as P

MESH = pl.DeviceIdType.MESH
NY = 4
NZ = 8
STEP = 8
F32 = jnp.float32
BF16 = jnp.bfloat16


def kept_of(row, col):
    return (col % 2) if row <= col // 2 else 1 - col % 2


def routes(count_i, count_j):
    there, back = [], []
    for row in range(count_i):
        for col in range(count_j):
            kept = kept_of(row, col)
            other = 1 - kept
            side = col // 2
            me = row * count_j + col
            there.append((me, side * count_j + 2 * row + other))
            pick = other if side == row else kept
            back.append((me, side * count_j + 2 * row + pick))
    return there, back


def ladder_kernel(
    vec, own, out,
    pairs, extra, work, acc, acc_own, acc_x, part, part_x, got_y, got_yx, got_z, got_zx, send_z, send_zx,
    zs, zr, ys, yr, xs, xr, rs, rr, rxs, rxr, ss, sr, sxs, sxr,
):
    row = lax.axis_index("pi")
    col = lax.axis_index("pj")
    y = lax.rem(col, NY)
    z = col // NY
    n = vec.shape[1]
    count = NY * NZ
    col_x = 2 * row + 1
    y_x = lax.rem(col_x, NY)
    z_x = col_x // NY

    def at(zz, yy):
        return (row, zz * NY + yy)

    def copy(src, dst, s, r, to):
        return pltpu.make_async_remote_copy(src, dst, s, r, device_id=to, device_id_type=MESH)

    barrier = pltpu.get_barrier_semaphore()

    def greet(k, _):
        pl.semaphore_signal(
            barrier, 1, device_id=(row, lax.rem(col + k, count)), device_id_type=MESH
        )
        return 0

    lax.fori_loop(1, count, greet, 0)
    pl.semaphore_wait(barrier, count - 1)

    def z_copy(k):
        to = lax.rem(z + k, NZ)
        return copy(own.at[0], pairs.at[y, z], zs.at[k], zr.at[k], at(to, y))

    for k in range(1, NZ):
        z_copy(k).start()

    def x_copy(k):
        return copy(own.at[1], extra, xs.at[k], xr, (row, lax.rem(col + k, count)))

    is_x = col == col_x

    @pl.when(is_x)
    def _():
        def go(k, _):
            x_copy(k).start()
            return 0

        lax.fori_loop(1, count, go, 0)

    pairs[y, z] = own[0]
    for k in range(1, NZ):
        copy(
            own.at[0], pairs.at[y, lax.rem(z + NZ - k, NZ)], zs.at[k], zr.at[k], at(z, y)
        ).wait_recv()

    def y_copy(k):
        return copy(pairs.at[y], pairs.at[y], ys.at[k], yr.at[k], at(z, lax.rem(y + k, NY)))

    for k in range(1, NY):
        y_copy(k).start()

    def first(block, index, slot, wide):
        lp = vec[pl.ds(pl.multiple_of(index * STEP * n, STEP * n), STEP * n), :]
        work[slot, :, 0 : wide * n] = jnp.dot(
            lp, block, preferred_element_type=F32
        ).astype(BF16)

    def second(index, slot, wide):
        lp = vec[pl.ds(pl.multiple_of(index * STEP * n, STEP * n), STEP * n), :]
        rows = []
        for p in range(wide):
            tiles = [
                work[slot, q * n : (q + 1) * n, p * n : (p + 1) * n] for q in range(STEP)
            ]
            rows.append(jnp.concatenate(tiles, axis=1))
        lhs = jnp.concatenate(rows, axis=0)
        acc[0 : wide * n, :] += jnp.dot(lhs, lp, preferred_element_type=F32)

    def group(yg, with_extra):
        wide = NZ + 1 if with_extra else NZ
        steps = n // STEP

        def block():
            tiles = [pairs[yg, k] for k in range(NZ)]
            if with_extra:
                tiles.append(extra[...])
            return jnp.concatenate(tiles, axis=1)

        acc[...] = jnp.zeros_like(acc)
        first(block(), 0, 0, wide)

        def step(index, _):
            slot = lax.rem(index, 2)
            first(block(), jnp.minimum(index + 1, steps - 1), 1 - slot, wide)
            second(index, slot, wide)
            return 0

        lax.fori_loop(0, steps, step, 0)

    def r_copy(k):
        return copy(
            part.at[k], got_y.at[k], rs.at[k], rr.at[k], at(z, lax.rem(y + NY - k, NY))
        )

    def y_wait(k):
        source = lax.rem(y + NY - k, NY)
        copy(pairs.at[y], pairs.at[source], ys.at[k], yr.at[k], at(z, y)).wait_recv()

    group(y, False)
    acc_own[...] = acc[0 : NZ * n, :]

    def turn(k, _):
        y_wait(k)
        group(lax.rem(y + NY - k, NY), False)
        part[k] = acc[0 : NZ * n, :].astype(BF16).reshape(NZ, n, n)
        r_copy(k).start()
        return 0

    lax.fori_loop(1, NY - 1, turn, 0)

    last = NY - 1
    y_wait(last)

    @pl.when(is_x)
    def _():
        extra[...] = own[1]

    @pl.when(jnp.logical_not(is_x))
    def _():
        x_copy(0).wait_recv()

    group(lax.rem(y + 1, NY), True)
    part[last] = acc[0 : NZ * n, :].astype(BF16).reshape(NZ, n, n)
    r_copy(last).start()
    part_x[...] = acc[NZ * n :, :].astype(BF16)
    acc_x[...] = acc[NZ * n :, :]

    on_y = y == y_x
    gap_y = lax.rem(y_x + NY - y, NY)

    def rx_copy(k):
        return copy(part_x, got_yx.at[k], rxs, rxr.at[k], at(z, y_x))

    @pl.when(jnp.logical_not(on_y))
    def _():
        rx_copy(gap_y).start()

    for k in range(1, NY):
        copy(part.at[k], got_y.at[k], rs.at[k], rr.at[k], at(z, y)).wait_recv()
    send_z[...] = (
        acc_own[...].reshape(NZ, n, n)
        + got_y[1].astype(F32) + got_y[2].astype(F32) + got_y[3].astype(F32)
    ).astype(BF16)

    def s_copy(k):
        to = lax.rem(z + k, NZ)
        return copy(send_z.at[to], got_z.at[k], ss.at[k], sr.at[k], at(to, y))

    for k in range(1, NZ):
        s_copy(k).start()

    on_x = jnp.logical_and(on_y, z == z_x)
    near_x = jnp.logical_and(on_y, z != z_x)
    gap_z = lax.rem(z_x + NZ - z, NZ)

    def sx_copy(k):
        return copy(send_zx, got_zx.at[k], sxs, sxr.at[k], at(z_x, y))

    @pl.when(on_y)
    def _():
        for k in range(1, NY):
            copy(part_x, got_yx.at[k], rxs, rxr.at[k], at(z, y)).wait_recv()
        acc_x[...] += (
            got_yx[1].astype(F32) + got_yx[2].astype(F32) + got_yx[3].astype(F32)
        )
        send_zx[...] = acc_x[...].astype(BF16)

    @pl.when(near_x)
    def _():
        sx_copy(gap_z).start()

    total = send_z[z].astype(F32)
    for k in range(1, NZ):
        copy(send_z.at[z], got_z.at[k], ss.at[k], sr.at[k], at(z, y)).wait_recv()
        total = total + got_z[k].astype(F32)
    out[0] = total
    out[1] = acc_x[...]

    @pl.when(on_x)
    def _():
        whole = acc_x[...]
        for k in range(1, NZ):
            copy(send_zx, got_zx.at[k], sxs, sxr.at[k], at(z, y)).wait_recv()
            whole = whole + got_zx[k].astype(F32)
        out[1] = whole

    for k in range(1, NZ):
        z_copy(k).wait_send()
        s_copy(k).wait_send()
    for k in range(1, NY):
        y_copy(k).wait_send()
        r_copy(k).wait_send()

    @pl.when(is_x)
    def _():
        def end(k, _):
            x_copy(k).wait_send()
            return 0

        lax.fori_loop(1, count, end, 0)

    @pl.when(jnp.logical_not(on_y))
    def _():
        rx_copy(gap_y).wait_send()

    @pl.when(near_x)
    def _():
        sx_copy(gap_z).wait_send()


def ladder_of(vectors, own):
    n = own.shape[-1]
    dma = pltpu.SemaphoreType.DMA
    vmem = pltpu.VMEM
    return pl.pallas_call(
        ladder_kernel,
        out_shape=jax.ShapeDtypeStruct((2, n, n), F32),
        in_specs=[pl.BlockSpec(memory_space=vmem)] * 2,
        out_specs=pl.BlockSpec(memory_space=vmem),
        scratch_shapes=[
            vmem((NY, NZ, n, n), BF16),
            vmem((n, n), BF16),
            vmem((2, STEP * n, (NZ + 1) * n), BF16),
            vmem(((NZ + 1) * n, n), F32),
            vmem((NZ * n, n), F32),
            vmem((n, n), F32),
            vmem((NY, NZ, n, n), BF16),
            vmem((n, n), BF16),
            vmem((NY, NZ, n, n), BF16),
            vmem((NY, n, n), BF16),
            vmem((NZ, n, n), BF16),
            vmem((NZ, n, n), BF16),
            vmem((NZ, n, n), BF16),
            vmem((n, n), BF16),
            dma((NZ,)), dma((NZ,)),
            dma((NY,)), dma((NY,)),
            dma((NY * NZ,)), dma,
            dma((NY,)), dma((NY,)),
            dma, dma((NY,)),
            dma((NZ,)), dma((NZ,)),
            dma, dma((NZ,)),
        ],
        compiler_params=pltpu.CompilerParams(
            collective_id=0, has_side_effects=True, vmem_limit_bytes=56 * 2**20
        ),
    )(vectors, own)


def shards(amplitudes, cholesky, other_terms):
    n = cholesky.shape[0]
    count_i = lax.axis_size("pi")
    count_j = lax.axis_size("pj")
    row = lax.axis_index("pi")
    col = lax.axis_index("pj")
    there, back = routes(count_i, count_j)
    side = col // 2
    diagonal = row == side
    second = jnp.where(row <= side, col % 2 == 1, col % 2 == 0)

    def pick(pair, which):
        return jnp.where(which, pair[1], pair[0])

    a = amplitudes[:, 0]
    o = other_terms[:, 0]
    a_kept, a_other = pick(a, second), pick(a, ~second)
    o_kept, o_other = pick(o, second), pick(o, ~second)
    axes = ("pi", "pj")
    a_in = lax.ppermute(a_other, axes, there)
    o_in = lax.ppermute(o_other, axes, there)
    mate = jnp.where(diagonal, a_kept, a_in).astype(F32)
    kept = a_kept.astype(F32) + mate.T
    extra = a_other.astype(F32) + a_in.astype(F32).T
    own = jnp.stack([kept, extra]).astype(BF16)
    vectors = jnp.transpose(cholesky, (2, 0, 1)).reshape(-1, n)
    ladder = ladder_of(vectors, own)
    o_mate = jnp.where(diagonal, o_kept, o_in)
    res_kept = o_kept + o_mate.T + 0.5 * ladder[0]
    res_extra = o_other + o_in.T + 0.5 * ladder[1]
    outgoing = jnp.where(diagonal, res_extra, res_kept)
    incoming = lax.ppermute(outgoing, axes, back).T
    keep_extra = jnp.logical_and(diagonal, col % 2 == 1)
    res_other = jnp.where(keep_extra, res_extra, incoming)
    low = jnp.where(second, res_other, res_kept)
    high = jnp.where(second, res_kept, res_other)
    return jnp.stack([low, high])[:, None]


def solution(mesh):
    return jax.shard_map(
        shards,
        mesh=mesh,
        in_specs=(P("pi", "pj", None, None), P(None, None, "pj"), P("pi", "pj", None, None)),
        out_specs=P("pi", "pj", None, None),
        check_vma=False,
    )
```

time: 868 us -> 183 us (0.21)
  waiting for transfers between devices: 666 us -> 10.9 us
  Pallas kernels: 0 us -> 136 us
  blocking collectives: 107 us -> 0 us
  starting transfers between devices: 72.2 us -> 21.5 us
  matrix products: 9.53 us -> 0 us
    all_to_all x4 -> x0, waiting for transfers between devices: 657 us -> none  [the longest x2 458 us: spread(): return lax.all_to_all(copies, axis, split_axis=0, concat_axis=0, tiled=True)]
    pallas_call x0 -> x1, Pallas kernels: none -> 136 us  [ladder_of(): pl.pallas_call(ladder_kernel, out_shape=jax.ShapeDtypeStruct((2, n, n), F...]
    all_to_all x2 -> x0, blocking collectives: 107 us -> none  [the longest x1 75.9 us: shards(): lax.all_to_all(sums.reshape(count_i, pair_i, count_j, block_j, width), 'p...]
    all_to_all x4 -> x0, starting transfers between devices: 57.4 us -> none  [the longest x1 34.3 us: shards(): lax.all_to_all(summed, 'pj', split_axis=1, concat_axis=1, tiled=True)]
    dot_general x2 -> x0, matrix products: 9.53 us -> none  [the longest x1 8.25 us: shards(): jnp.einsum('kcap,kbdp->cdba', from_i, from_j, preferred_element_type=jnp....]
    ppermute x2 -> x3, starting transfers between devices: 14.8 us -> 21.5 us  [the longest x1 14.6 us: shards(): a_in = lax.ppermute(a_other, axes, there)]
  transfers between devices with their start and end apart: 6 -> 3, of which waited for: 6 -> 1; matrix products, arithmetic and copies ran while one was open for 1% -> 5% of each run, Pallas kernels for 0% -> 75%
where the time goes in v2:
time: 183 us; the launch traced here: 181 us
  Pallas kernels  136 us (74%)
  starting transfers between devices  21.5 us (12%)
  waiting for transfers between devices  10.9 us (6%)
  local copies, waits for them, and re-layouts  7.43 us (4%)
  other arithmetic  4.79 us (3%)
    pallas_call x1, Pallas kernels, ladder_of(): pl.pallas_call(ladder_kernel, out_shape=jax.ShapeDtypeStruct((2, n, n), F...  136 us
    ppermute x1, starting transfers between devices, shards(): a_in = lax.ppermute(a_other, axes, there)  14.6 us
    ppermute x1, waiting for transfers between devices, shards(): incoming = lax.ppermute(outgoing, axes, back).T  10.9 us
    transpose x1, local copies, waits for them, and re-layouts, shards(): vectors = jnp.transpose(cholesky, (2, 0, 1)).reshape(-1, n)  6.67 us
    ppermute x1, starting transfers between devices, shards(): incoming = lax.ppermute(outgoing, axes, back).T  4.94 us
  transfers between devices with their start and end apart: 3, of which 1 were waited for; matrix products, arithmetic and copies ran while one was open for 5% of the time, Pallas kernels for 75%

profile of v2, /device:TPU:7, one launch (start us, length us, event | category | flops | bytes accessed | tf_op | source)
XLA Modules:
  0.0 180.8 jit_solution(3661615870979781679)
XLA Ops:
  0.0 0.8 select_bitcast_fusion.5
  0.8 0.1 copy.11
  0.9 14.6 %collective-permute-start.1 = (bf16[128,128]{0,1:T(8,128)(2,1)S(1)}, bf16[128,128]{0,1:T(8,128)(2,1)S(1)}, u32[]{:S(2)}, u32[]{:S(2)}) collective-permute-start(bf16[128,128]{0,1:T(8,128)(2,1)S(1)} %copy.11), channel_id=1, source_target_pairs={{0,1},{1,0},{2,33},{3,32},{4,65},{5,64},{6,97},{7,96},{8,129},{9,1... | collective-permute-start | bytes 98312 | tf_op jit(solution)/shard_map/ppermute | solution.py:314
  15.5 0.9 select_bitcast_fusion.3
  16.4 1.9 %collective-permute-start = (f32[128,128]{1,0:T(8,128)S(1)}, f32[128,128]{1,0:T(8,128)S(1)}, u32[]{:S(2)}, u32[]{:S(2)}) collective-permute-start(f32[128,128]{1,0:T(8,128)S(1)} %get-tuple-element.9), channel_id=1, source_target_pairs={{0,1},{1,0},{2,33},{3,32},{4,65},{5,64},{6,97},{7,96},{8,129},{9,1... | collective-permute-start | bytes 196616 | tf_op jit(solution)/shard_map/ppermute | solution.py:315
  18.4 0.1 copy.18
  18.5 0.1 copy.19
  18.6 0.1 copy.13
  18.7 6.7 %copy.9 = bf16[128,128,128]{2,1,0:T(8,128)(2,1)} copy(bf16[128,128,128]{0,2,1:T(8,128)(2,1)} %bitcast.50) | data formatting | bytes 8388608 | tf_op jit(solution)/shard_map/transpose | solution.py:320
  25.4 0.1 copy.14
  25.5 0.0 collective-permute-done.1
  25.5 0.6 pad_maximum_fusion.own
  26.1 136.1 %shard_map.37 = f32[2,128,128]{2,1,0:T(8,128)} custom-call(bf16[16384,128]{1,0:T(8,128)(2,1)} %bitcast.49, bf16[2,128,128]{2,1,0:T(8,128)(2,1)} %pad_maximum_fusion.own), custom_call_target="tpu_custom_call" | custom-call | tf_op jit(solution)/shard_map/pallas_call | solution.py:261
  162.2 0.0 collective-permute-done
  162.2 0.1 copy.15
  162.3 0.1 copy.8
  162.4 0.9 broadcast_select_fusion
  163.3 4.9 %collective-permute-start.2 = (f32[128,128]{1,0:T(8,128)S(1)}, f32[128,128]{1,0:T(8,128)S(1)}, u32[]{:S(2)}, u32[]{:S(2)}) collective-permute-start(f32[128,128]{1,0:T(8,128)S(1)} %get-tuple-element.5), channel_id=1, source_target_pairs={{0,1},{1,0},{2,32},{3,33},{4,64},{5,65},{6,96},{7,97},{8,128},{9,1... | collective-permute-start | bytes 196616 | tf_op jit(solution)/shard_map/ppermute | solution.py:326
  168.3 10.9 %collective-permute-done.2 = f32[128,128]{1,0:T(8,128)S(1)} collective-permute-done((f32[128,128]{1,0:T(8,128)S(1)}, f32[128,128]{1,0:T(8,128)S(1)}, u32[]{:S(2)}, u32[]{:S(2)}) %collective-permute-start.2) | collective-permute-done | bytes 65568 | tf_op jit(solution)/shard_map/ppermute | solution.py:326
  179.1 0.1 copy.16
  179.2 0.9 select_bitcast_fusion.1
  180.1 0.7 maximum_bitcast_fusion
  (3 shorter events, 0.0 us)
Async XLA Ops:
  0.9 24.6 %collective-permute-start.1 = (bf16[128,128]{0,1:T(8,128)(2,1)S(1)}, bf16[128,128]{0,1:T(8,128)(2,1)S(1)}, u32[]{:S(2)}, u32[]{:S(2)}) collective-permute-start(bf16[128,128]{0,1:T(8,128)(2,1)S(1)} %copy.11), channel_id=1, source_target_pairs={{0,1},{1,0},{2,33},{3,32},{4,65},{5,64},{6,97},{7,96},{8,129},{9,1... | collective-permute-start | bytes 98312 | tf_op jit(solution)/shard_map/ppermute | solution.py:314
  16.4 145.8 %collective-permute-start = (f32[128,128]{1,0:T(8,128)S(1)}, f32[128,128]{1,0:T(8,128)S(1)}, u32[]{:S(2)}, u32[]{:S(2)}) collective-permute-start(f32[128,128]{1,0:T(8,128)S(1)} %get-tuple-element.9), channel_id=1, source_target_pairs={{0,1},{1,0},{2,33},{3,32},{4,65},{5,64},{6,97},{7,96},{8,129},{9,1... | collective-permute-start | bytes 196616 | tf_op jit(solution)/shard_map/ppermute | solution.py:315
  163.3 15.8 %collective-permute-start.2 = (f32[128,128]{1,0:T(8,128)S(1)}, f32[128,128]{1,0:T(8,128)S(1)}, u32[]{:S(2)}, u32[]{:S(2)}) collective-permute-start(f32[128,128]{1,0:T(8,128)S(1)} %get-tuple-element.5), channel_id=1, source_target_pairs={{0,1},{1,0},{2,32},{3,33},{4,64},{5,65},{6,96},{7,97},{8,128},{9,1... | collective-permute-start | bytes 196616 | tf_op jit(solution)/shard_map/ppermute | solution.py:326

commit v3 on v2

v3 whole, which is shorter than its diff:
```python
import jax
import jax.numpy as jnp
from jax import lax
from jax.experimental import pallas as pl
from jax.experimental.pallas import tpu as pltpu
from jax.sharding import PartitionSpec as P

MESH = pl.DeviceIdType.MESH
NY = 4
NZ = 8
STEP = 16
F32 = jnp.float32
BF16 = jnp.bfloat16


def kept_of(row, col):
    return (col % 2) if row <= col // 2 else 1 - col % 2


def routes(count_i, count_j):
    there, back = [], []
    for row in range(count_i):
        for col in range(count_j):
            kept = kept_of(row, col)
            other = 1 - kept
            side = col // 2
            me = row * count_j + col
            there.append((me, side * count_j + 2 * row + other))
            pick = other if side == row else kept
            back.append((me, side * count_j + 2 * row + pick))
    return there, back


def ladder_kernel(
    vec, own, out,
    pairs, extra, work, acc, acc_own, acc_x, part, part_x, got_z, got_zx, total, send_y, got_y, send_yx, got_yx,
    hs, hr, zs, zr, fs, fr, xs, xr, rs, rr, rxs, rxr, ss, sr, sxs, sxr,
):
    row = lax.axis_index("pi")
    col = lax.axis_index("pj")
    y = lax.rem(col, NY)
    z = col // NY
    n = vec.shape[1]
    count = NY * NZ
    steps = n // STEP
    col_x = 2 * row + 1
    y_x = lax.rem(col_x, NY)
    z_x = col_x // NY

    def at(zz, yy):
        return (row, zz * NY + yy)

    def bits(v):
        return (v % 2, (v // 2) % 2, v // 4)

    def across(v):
        return sum(((a + b) % 2) * 2**k for k, (a, b) in enumerate(zip(bits(z), bits(v))))

    def ahead(k):
        return lax.rem(y + k, NY)

    def copy(src, dst, s, r, to):
        return pltpu.make_async_remote_copy(src, dst, s, r, device_id=to, device_id_type=MESH)

    barrier = pltpu.get_barrier_semaphore()

    def greet(k, _):
        pl.semaphore_signal(
            barrier, 1, device_id=(row, lax.rem(col + k, count)), device_id_type=MESH
        )
        return 0

    lax.fori_loop(1, count, greet, 0)
    pl.semaphore_wait(barrier, count - 1)

    def h_copy(k):
        return copy(own.at[0], pairs.at[0, y], hs.at[k], hr.at[k], at(z, ahead(k)))

    def z_copy(k):
        return copy(own.at[0], pairs.at[k, y], zs.at[k], zr.at[k], at(across(k), y))

    def f_copy(k, j):
        m = k * NY + j
        return copy(pairs.at[k, y], pairs.at[k, y], fs.at[m], fr.at[m], at(z, ahead(j)))

    def x_copy(k):
        return copy(own.at[1], extra, xs.at[k], xr, (row, lax.rem(col + k, count)))

    def r_copy(k):
        return copy(part.at[k], got_z.at[k], rs.at[k], rr.at[k], at(across(k), y))

    def s_copy(k):
        return copy(send_y.at[ahead(k)], got_y.at[k], ss.at[k], sr.at[k], at(z, ahead(k)))

    for k in range(1, NY):
        h_copy(k).start()
    for k in range(1, NZ):
        z_copy(k).start()
    is_x = col == col_x

    @pl.when(is_x)
    def _():
        def go(k, _):
            x_copy(k).start()
            return 0

        lax.fori_loop(1, count, go, 0)
        extra[...] = own[1]

    pairs[0, y] = own[0]

    def forward(ks):
        for k in ks:
            z_copy(k).wait_recv()
            for j in range(1, NY):
                f_copy(k, j).start()

    def first(block, index, slot, wide):
        lp = vec[pl.ds(pl.multiple_of(index * STEP * n, STEP * n), STEP * n), :]
        work[slot, :, 0 : wide * n] = jnp.dot(
            lp, block, preferred_element_type=F32
        ).astype(BF16)

    def second(index, slot, wide):
        lp = vec[pl.ds(pl.multiple_of(index * STEP * n, STEP * n), STEP * n), :]
        rows = []
        for p in range(wide):
            tiles = [
                work[slot, q * n : (q + 1) * n, p * n : (p + 1) * n] for q in range(STEP)
            ]
            rows.append(jnp.concatenate(tiles, axis=1))
        lhs = jnp.concatenate(rows, axis=0)
        acc[0 : wide * n, :] += jnp.dot(lhs, lp, preferred_element_type=F32)

    def group(ks, with_extra=False, beside=None):
        wide = len(ks) * NY + int(with_extra)

        def block():
            tiles = [pairs[k, yy] for k in ks for yy in range(NY)]
            if with_extra:
                tiles.append(extra[...])
            return jnp.concatenate(tiles, axis=1)

        acc[...] = jnp.zeros_like(acc)
        first(block(), 0, 0, wide)

        def step(index, _):
            slot = lax.rem(index, 2)
            if beside is not None:
                pl.when(index == steps // 2)(beside)
            first(block(), jnp.minimum(index + 1, steps - 1), 1 - slot, wide)
            second(index, slot, wide)
            return 0

        lax.fori_loop(0, steps, step, 0)

    def ready(k):
        for j in range(1, NY):
            m = k * NY + j
            source = lax.rem(y + NY - j, NY)
            copy(
                pairs.at[k, y], pairs.at[k, source], fs.at[m], fr.at[m], at(z, ahead(j))
            ).wait_recv()

    def hand(k, at_row):
        rows = acc[at_row * NY * n : (at_row + 1) * NY * n, :]
        part[k] = rows.astype(BF16).reshape(NY, n, n)
        r_copy(k).start()

    for k in range(1, NY):
        source = lax.rem(y + NY - k, NY)
        copy(own.at[0], pairs.at[0, source], hs.at[k], hr.at[k], at(z, ahead(k))).wait_recv()
    group((0,), beside=lambda: forward((1, 2, 3)))
    acc_own[...] = acc[0 : NY * n, :]
    forward((4, 5, 6, 7))

    ready(2)
    ready(3)

    @pl.when(jnp.logical_not(is_x))
    def _():
        x_copy(1).wait_recv()

    group((2, 3), with_extra=True)
    hand(2, 0)
    hand(3, 1)
    acc_x[...] = acc[2 * NY * n :, :]
    part_x[...] = acc_x[...].astype(BF16)
    on_z = z == z_x
    far_z = z != z_x
    gap_z = across(z_x)

    def rx_copy(k):
        return copy(part_x, got_zx.at[k], rxs, rxr.at[k], at(z_x, y))

    @pl.when(far_z)
    def _():
        rx_copy(gap_z).start()

    def turn(t, _):
        k = 4 + 2 * t
        ready(k)
        ready(k + 1)
        group((k, k + 1))
        hand(k, 0)
        hand(k + 1, 1)
        return 0

    lax.fori_loop(0, 2, turn, 0)

    on_x = jnp.logical_and(on_z, y == y_x)
    near_x = jnp.logical_and(on_z, y != y_x)
    gap_y = lax.rem(y_x + NY - y, NY)

    def sx_copy(k):
        return copy(send_yx, got_yx.at[k], sxs, sxr.at[k], at(z, y_x))

    @pl.when(on_z)
    def _():
        whole = acc_x[...]
        for k in range(1, NZ):
            copy(part_x, got_zx.at[k], rxs, rxr.at[k], at(across(k), y)).wait_recv()
            whole = whole + got_zx[k].astype(F32)
        acc_x[...] = whole
        send_yx[...] = whole.astype(BF16)

    @pl.when(near_x)
    def _():
        sx_copy(gap_y).start()

    ready(1)
    group((1,))
    hand(1, 0)
    total[...] = acc_own[...].reshape(NY, n, n)
    for k in (2, 3, 4, 5, 6, 7, 1):
        r_copy(k).wait_recv()
        total[...] += got_z[k].astype(F32)
    send_y[...] = total[...].astype(BF16)
    for k in range(1, NY):
        s_copy(k).start()
    out[1] = acc_x[...]

    @pl.when(on_x)
    def _():
        whole = acc_x[...]
        for k in range(1, NY):
            copy(send_yx, got_yx.at[k], sxs, sxr.at[k], at(z, ahead(k))).wait_recv()
            whole = whole + got_yx[k].astype(F32)
        out[1] = whole

    ladder = total[y]
    for k in range(1, NY):
        s_copy(k).wait_recv()
        ladder = ladder + got_y[k].astype(F32)
    out[0] = ladder

    for k in range(1, NZ):
        z_copy(k).wait_send()
        r_copy(k).wait_send()
        for j in range(1, NY):
            f_copy(k, j).wait_send()
    for k in range(1, NY):
        h_copy(k).wait_send()
        s_copy(k).wait_send()

    @pl.when(is_x)
    def _():
        def end(k, _):
            x_copy(k).wait_send()
            return 0

        lax.fori_loop(1, count, end, 0)

    @pl.when(far_z)
    def _():
        rx_copy(gap_z).wait_send()

    @pl.when(near_x)
    def _():
        sx_copy(gap_y).wait_send()


def ladder_of(vectors, own):
    n = own.shape[-1]
    dma = pltpu.SemaphoreType.DMA
    vmem = pltpu.VMEM
    wide = 2 * NY + 1
    return pl.pallas_call(
        ladder_kernel,
        out_shape=jax.ShapeDtypeStruct((2, n, n), F32),
        in_specs=[pl.BlockSpec(memory_space=vmem)] * 2,
        out_specs=pl.BlockSpec(memory_space=vmem),
        scratch_shapes=[
            vmem((NZ, NY, n, n), BF16),
            vmem((n, n), BF16),
            vmem((2, STEP * n, wide * n), BF16),
            vmem((wide * n, n), F32),
            vmem((NY * n, n), F32),
            vmem((n, n), F32),
            vmem((NZ, NY, n, n), BF16),
            vmem((n, n), BF16),
            vmem((NZ, NY, n, n), BF16),
            vmem((NZ, n, n), BF16),
            vmem((NY, n, n), F32),
            vmem((NY, n, n), BF16),
            vmem((NY, n, n), BF16),
            vmem((n, n), BF16),
            vmem((NY, n, n), BF16),
            dma((NY,)), dma((NY,)),
            dma((NZ,)), dma((NZ,)),
            dma((NY * NZ,)), dma((NY * NZ,)),
            dma((NY * NZ,)), dma,
            dma((NZ,)), dma((NZ,)),
            dma, dma((NZ,)),
            dma((NY,)), dma((NY,)),
            dma, dma((NY,)),
        ],
        compiler_params=pltpu.CompilerParams(
            collective_id=0, has_side_effects=True, vmem_limit_bytes=56 * 2**20
        ),
    )(vectors, own)


def shards(amplitudes, cholesky, other_terms):
    n = cholesky.shape[0]
    count_i = lax.axis_size("pi")
    count_j = lax.axis_size("pj")
    row = lax.axis_index("pi")
    col = lax.axis_index("pj")
    there, back = routes(count_i, count_j)
    side = col // 2
    diagonal = row == side
    second = jnp.where(row <= side, col % 2 == 1, col % 2 == 0)

    def pick(pair, which):
        return jnp.where(which, pair[1], pair[0])

    a = amplitudes[:, 0]
    o = other_terms[:, 0]
    a_kept, a_other = pick(a, second), pick(a, ~second)
    o_kept, o_other = pick(o, second), pick(o, ~second)
    axes = ("pi", "pj")
    a_in = lax.ppermute(a_other, axes, there)
    o_in = lax.ppermute(o_other, axes, there)
    mate = jnp.where(diagonal, a_kept, a_in).astype(F32)
    kept = a_kept.astype(F32) + mate.T
    extra = a_other.astype(F32) + a_in.astype(F32).T
    own = jnp.stack([kept, extra]).astype(BF16)
    vectors = jnp.transpose(cholesky, (2, 0, 1)).reshape(-1, n)
    ladder = ladder_of(vectors, own)
    o_mate = jnp.where(diagonal, o_kept, o_in)
    res_kept = o_kept + o_mate.T + 0.5 * ladder[0]
    res_extra = o_other + o_in.T + 0.5 * ladder[1]
    outgoing = jnp.where(diagonal, res_extra, res_kept)
    incoming = lax.ppermute(outgoing, axes, back).T
    keep_extra = jnp.logical_and(diagonal, col % 2 == 1)
    res_other = jnp.where(keep_extra, res_extra, incoming)
    low = jnp.where(second, res_other, res_kept)
    high = jnp.where(second, res_kept, res_other)
    return jnp.stack([low, high])[:, None]


def solution(mesh):
    return jax.shard_map(
        shards,
        mesh=mesh,
        in_specs=(P("pi", "pj", None, None), P(None, None, "pj"), P("pi", "pj", None, None)),
        out_specs=P("pi", "pj", None, None),
        check_vma=False,
    )
```

time: 183 us -> 167 us (0.913)
  the two profiles are of different devices: /device:TPU:7 before, /device:TPU:96 now
where the time goes in v3:
time: 167 us; the launch traced here: 166 us
  Pallas kernels  123 us (74%)
  starting transfers between devices  17.4 us (10%)
  waiting for transfers between devices  12.9 us (8%)
  local copies, waits for them, and re-layouts  7.43 us (4%)
  other arithmetic  4.79 us (3%)
    pallas_call x1, Pallas kernels, ladder_of(): pl.pallas_call(ladder_kernel, out_shape=jax.ShapeDtypeStruct((2, n, n), F...  123 us
    ppermute x1, starting transfers between devices, shards(): a_in = lax.ppermute(a_other, axes, there)  13.6 us
    ppermute x1, waiting for transfers between devices, shards(): incoming = lax.ppermute(outgoing, axes, back).T  12.9 us
    transpose x1, local copies, waits for them, and re-layouts, shards(): vectors = jnp.transpose(cholesky, (2, 0, 1)).reshape(-1, n)  6.67 us
  transfers between devices with their start and end apart: 3, of which 1 were waited for; matrix products, arithmetic and copies ran while one was open for 5% of the time, Pallas kernels for 74%

profile of v3, /device:TPU:96, one launch (start us, length us, event | category | flops | bytes accessed | tf_op | source)
XLA Modules:
  0.0 166.1 jit_solution(1883215040562005700)
XLA Ops:
  0.0 0.8 select_bitcast_fusion.5
  0.8 0.1 copy.11
  0.9 13.6 %collective-permute-start.1 = (bf16[128,128]{0,1:T(8,128)(2,1)S(1)}, bf16[128,128]{0,1:T(8,128)(2,1)S(1)}, u32[]{:S(2)}, u32[]{:S(2)}) collective-permute-start(bf16[128,128]{0,1:T(8,128)(2,1)S(1)} %copy.11), channel_id=1, source_target_pairs={{0,1},{1,0},{2,33},{3,32},{4,65},{5,64},{6,97},{7,96},{8,129},{9,1... | collective-permute-start | bytes 98312 | tf_op jit(solution)/shard_map/ppermute | solution.py:343
  14.5 0.9 select_bitcast_fusion.3
  15.4 1.9 %collective-permute-start = (f32[128,128]{1,0:T(8,128)S(1)}, f32[128,128]{1,0:T(8,128)S(1)}, u32[]{:S(2)}, u32[]{:S(2)}) collective-permute-start(f32[128,128]{1,0:T(8,128)S(1)} %get-tuple-element.9), channel_id=1, source_target_pairs={{0,1},{1,0},{2,33},{3,32},{4,65},{5,64},{6,97},{7,96},{8,129},{9,1... | collective-permute-start | bytes 196616 | tf_op jit(solution)/shard_map/ppermute | solution.py:344
  17.3 0.1 copy.18
  17.4 0.1 copy.19
  17.6 0.1 copy.13
  17.7 6.7 %copy.9 = bf16[128,128,128]{2,1,0:T(8,128)(2,1)} copy(bf16[128,128,128]{0,2,1:T(8,128)(2,1)} %bitcast.50) | data formatting | bytes 8388608 | tf_op jit(solution)/shard_map/transpose | solution.py:349
  24.3 0.1 copy.14
  24.4 0.0 collective-permute-done.1
  24.5 0.6 pad_maximum_fusion.own
  25.1 123.4 %shard_map.37 = f32[2,128,128]{2,1,0:T(8,128)} custom-call(bf16[16384,128]{1,0:T(8,128)(2,1)} %bitcast.49, bf16[2,128,128]{2,1,0:T(8,128)(2,1)} %pad_maximum_fusion.own), custom_call_target="tpu_custom_call" | custom-call | tf_op jit(solution)/shard_map/pallas_call | solution.py:288
  148.5 0.0 collective-permute-done
  148.5 0.1 copy.15
  148.6 0.1 copy.8
  148.7 0.9 broadcast_select_fusion
  149.6 1.9 %collective-permute-start.2 = (f32[128,128]{1,0:T(8,128)S(1)}, f32[128,128]{1,0:T(8,128)S(1)}, u32[]{:S(2)}, u32[]{:S(2)}) collective-permute-start(f32[128,128]{1,0:T(8,128)S(1)} %get-tuple-element.5), channel_id=1, source_target_pairs={{0,1},{1,0},{2,32},{3,33},{4,64},{5,65},{6,96},{7,97},{8,128},{9,1... | collective-permute-start | bytes 196616 | tf_op jit(solution)/shard_map/ppermute | solution.py:355
  151.6 12.9 %collective-permute-done.2 = f32[128,128]{1,0:T(8,128)S(1)} collective-permute-done((f32[128,128]{1,0:T(8,128)S(1)}, f32[128,128]{1,0:T(8,128)S(1)}, u32[]{:S(2)}, u32[]{:S(2)}) %collective-permute-start.2) | collective-permute-done | bytes 65568 | tf_op jit(solution)/shard_map/ppermute | solution.py:355
  164.5 0.1 copy.16
  164.6 0.9 select_bitcast_fusion.1
  165.5 0.7 maximum_bitcast_fusion
  (3 shorter events, 0.0 us)
Async XLA Ops:
  0.9 23.5 %collective-permute-start.1 = (bf16[128,128]{0,1:T(8,128)(2,1)S(1)}, bf16[128,128]{0,1:T(8,128)(2,1)S(1)}, u32[]{:S(2)}, u32[]{:S(2)}) collective-permute-start(bf16[128,128]{0,1:T(8,128)(2,1)S(1)} %copy.11), channel_id=1, source_target_pairs={{0,1},{1,0},{2,33},{3,32},{4,65},{5,64},{6,97},{7,96},{8,129},{9,1... | collective-permute-start | bytes 98312 | tf_op jit(solution)/shard_map/ppermute | solution.py:343
  15.4 133.1 %collective-permute-start = (f32[128,128]{1,0:T(8,128)S(1)}, f32[128,128]{1,0:T(8,128)S(1)}, u32[]{:S(2)}, u32[]{:S(2)}) collective-permute-start(f32[128,128]{1,0:T(8,128)S(1)} %get-tuple-element.9), channel_id=1, source_target_pairs={{0,1},{1,0},{2,33},{3,32},{4,65},{5,64},{6,97},{7,96},{8,129},{9,1... | collective-permute-start | bytes 196616 | tf_op jit(solution)/shard_map/ppermute | solution.py:344
  149.6 14.9 %collective-permute-start.2 = (f32[128,128]{1,0:T(8,128)S(1)}, f32[128,128]{1,0:T(8,128)S(1)}, u32[]{:S(2)}, u32[]{:S(2)}) collective-permute-start(f32[128,128]{1,0:T(8,128)S(1)} %get-tuple-element.5), channel_id=1, source_target_pairs={{0,1},{1,0},{2,32},{3,33},{4,64},{5,65},{6,96},{7,97},{8,128},{9,1... | collective-permute-start | bytes 196616 | tf_op jit(solution)/shard_map/ppermute | solution.py:355

commit v4 on v3

--- a/solution.py
+++ b/solution.py
@@ -17,24 +17,19 @@
     return (col % 2) if row <= col // 2 else 1 - col % 2
 
 
-def routes(count_i, count_j):
-    there, back = [], []
+def route(count_i, count_j):
+    there = []
     for row in range(count_i):
         for col in range(count_j):
-            kept = kept_of(row, col)
-            other = 1 - kept
-            side = col // 2
-            me = row * count_j + col
-            there.append((me, side * count_j + 2 * row + other))
-            pick = other if side == row else kept
-            back.append((me, side * count_j + 2 * row + pick))
-    return there, back
+            other = 1 - kept_of(row, col)
+            there.append((row * count_j + col, (col // 2) * count_j + 2 * row + other))
+    return there
 
 
 def ladder_kernel(
-    vec, own, out,
-    pairs, extra, work, acc, acc_own, acc_x, part, part_x, got_z, got_zx, total, send_y, got_y, send_yx, got_yx,
-    hs, hr, zs, zr, fs, fr, xs, xr, rs, rr, rxs, rxr, ss, sr, sxs, sxr,
+    vec, own, base, out,
+    pairs, extra, work, acc, acc_own, acc_x, part, part_x, got_z, got_zx, total, send_y, got_y, send_yx, got_yx, done, got_m,
+    hs, hr, zs, zr, fs, fr, xs, xr, rs, rr, rxs, rxr, ss, sr, sxs, sxr, ms, mr,
 ):
     row = lax.axis_index("pi")
     col = lax.axis_index("pj")
@@ -46,6 +41,11 @@
     col_x = 2 * row + 1
     y_x = lax.rem(col_x, NY)
     z_x = col_x // NY
+    side = col // 2
+    kept = (col % 2 + (row - side + 15) // 16) % 2
+    is_x = col == col_x
+    off = row != side
+    is_y = jnp.logical_and(row == side, col != col_x)
 
     def at(zz, yy):
         return (row, zz * NY + yy)
@@ -71,7 +71,16 @@
         return 0
 
     lax.fori_loop(1, count, greet, 0)
-    pl.semaphore_wait(barrier, count - 1)
+
+    @pl.when(off)
+    def _():
+        for k in range(2):
+            pl.semaphore_signal(
+                barrier, 1, device_id=(side, 2 * row + k), device_id_type=MESH
+            )
+
+    gap = row - side
+    pl.semaphore_wait(barrier, count - 1 + 2 * ((gap * gap + 255) // 256))
 
     def h_copy(k):
         return copy(own.at[0], pairs.at[0, y], hs.at[k], hr.at[k], at(z, ahead(k)))
@@ -96,7 +105,6 @@
         h_copy(k).start()
     for k in range(1, NZ):
         z_copy(k).start()
-    is_x = col == col_x
 
     @pl.when(is_x)
     def _():
@@ -148,11 +156,12 @@
             slot = lax.rem(index, 2)
             if beside is not None:
                 pl.when(index == steps // 2)(beside)
-            first(block(), jnp.minimum(index + 1, steps - 1), 1 - slot, wide)
+            first(block(), index + 1, 1 - slot, wide)
             second(index, slot, wide)
             return 0
 
-        lax.fori_loop(0, steps, step, 0)
+        lax.fori_loop(0, steps - 1, step, 0)
+        second(steps - 1, (steps - 1) % 2, wide)
 
     def ready(k):
         for j in range(1, NY):
@@ -208,7 +217,6 @@
 
     lax.fori_loop(0, 2, turn, 0)
 
-    on_x = jnp.logical_and(on_z, y == y_x)
     near_x = jnp.logical_and(on_z, y != y_x)
     gap_y = lax.rem(y_x + NY - y, NY)
 
@@ -238,21 +246,35 @@
     send_y[...] = total[...].astype(BF16)
     for k in range(1, NY):
         s_copy(k).start()
-    out[1] = acc_x[...]
-
-    @pl.when(on_x)
+
+    def m_copy(to):
+        return copy(done, got_m, ms, mr, to)
+
+    mate = (side, 2 * row + kept)
+    sibling = (row, 2 * row)
+
+    @pl.when(is_x)
     def _():
         whole = acc_x[...]
+
         for k in range(1, NY):
             copy(send_yx, got_yx.at[k], sxs, sxr.at[k], at(z, ahead(k))).wait_recv()
             whole = whole + got_yx[k].astype(F32)
-        out[1] = whole
+        done[...] = base[1] + 0.5 * whole
+        m_copy(sibling).start()
+        out[0] = done[...]
 
     ladder = total[y]
     for k in range(1, NY):
         s_copy(k).wait_recv()
         ladder = ladder + got_y[k].astype(F32)
-    out[0] = ladder
+    finished = base[0] + 0.5 * ladder
+    out[kept] = finished
+
+    @pl.when(off)
+    def _():
+        done[...] = finished
+        m_copy(mate).start()
 
     for k in range(1, NZ):
         z_copy(k).wait_send()
@@ -279,8 +301,22 @@
     def _():
         sx_copy(gap_y).wait_send()
 
-
-def ladder_of(vectors, own):
+    @pl.when(is_x)
+    def _():
+        m_copy(sibling).wait_send()
+
+    @pl.when(off)
+    def _():
+        m_copy(mate).wait()
+        out[1 - kept] = got_m[...].T
+
+    @pl.when(is_y)
+    def _():
+        m_copy((row, col_x)).wait_recv()
+        out[1] = got_m[...].T
+
+
+def ladder_of(vectors, own, base):
     n = own.shape[-1]
     dma = pltpu.SemaphoreType.DMA
     vmem = pltpu.VMEM
@@ -288,7 +324,7 @@
     return pl.pallas_call(
         ladder_kernel,
         out_shape=jax.ShapeDtypeStruct((2, n, n), F32),
-        in_specs=[pl.BlockSpec(memory_space=vmem)] * 2,
+        in_specs=[pl.BlockSpec(memory_space=vmem)] * 3,
         out_specs=pl.BlockSpec(memory_space=vmem),
         scratch_shapes=[
             vmem((NZ, NY, n, n), BF16),
@@ -306,6 +342,8 @@
             vmem((NY, n, n), BF16),
             vmem((n, n), BF16),
             vmem((NY, n, n), BF16),
+            vmem((n, n), F32),
+            vmem((n, n), F32),
             dma((NY,)), dma((NY,)),
             dma((NZ,)), dma((NZ,)),
             dma((NY * NZ,)), dma((NY * NZ,)),
@@ -314,11 +352,12 @@
             dma, dma((NZ,)),
             dma((NY,)), dma((NY,)),
             dma, dma((NY,)),
+            dma, dma,
         ],
         compiler_params=pltpu.CompilerParams(
             collective_id=0, has_side_effects=True, vmem_limit_bytes=56 * 2**20
         ),
-    )(vectors, own)
+    )(vectors, own, base)
 
 
 def shards(amplitudes, cholesky, other_terms):
@@ -327,7 +366,6 @@
     count_j = lax.axis_size("pj")
     row = lax.axis_index("pi")
     col = lax.axis_index("pj")
-    there, back = routes(count_i, count_j)
     side = col // 2
     diagonal = row == side
     second = jnp.where(row <= side, col % 2 == 1, col % 2 == 0)
@@ -335,29 +373,14 @@
     def pick(pair, which):
         return jnp.where(which, pair[1], pair[0])
 
-    a = amplitudes[:, 0]
-    o = other_terms[:, 0]
-    a_kept, a_other = pick(a, second), pick(a, ~second)
-    o_kept, o_other = pick(o, second), pick(o, ~second)
-    axes = ("pi", "pj")
-    a_in = lax.ppermute(a_other, axes, there)
-    o_in = lax.ppermute(o_other, axes, there)
-    mate = jnp.where(diagonal, a_kept, a_in).astype(F32)
-    kept = a_kept.astype(F32) + mate.T
-    extra = a_other.astype(F32) + a_in.astype(F32).T
-    own = jnp.stack([kept, extra]).astype(BF16)
+    a = amplitudes[:, 0].astype(F32)
+    both = jnp.stack([a, other_terms[:, 0]], axis=1)
+    kept, other = pick(both, second), pick(both, ~second)
+    received = lax.ppermute(other, ("pi", "pj"), route(count_i, count_j))
+    mate = jnp.where(diagonal, kept, received)
+    sums = jnp.stack([kept + mate.swapaxes(1, 2), other + received.swapaxes(1, 2)])
     vectors = jnp.transpose(cholesky, (2, 0, 1)).reshape(-1, n)
-    ladder = ladder_of(vectors, own)
-    o_mate = jnp.where(diagonal, o_kept, o_in)
-    res_kept = o_kept + o_mate.T + 0.5 * ladder[0]
-    res_extra = o_other + o_in.T + 0.5 * ladder[1]
-    outgoing = jnp.where(diagonal, res_extra, res_kept)
-    incoming = lax.ppermute(outgoing, axes, back).T
-    keep_extra = jnp.logical_and(diagonal, col % 2 == 1)
-    res_other = jnp.where(keep_extra, res_extra, incoming)
-    low = jnp.where(second, res_other, res_kept)
-    high = jnp.where(second, res_kept, res_other)
-    return jnp.stack([low, high])[:, None]
+    return ladder_of(vectors, sums[:, 0].astype(BF16), sums[:, 1])[:, None]
 
 
 def solution(mesh):

time: 167 us -> 160 us (0.958)
  the two profiles are of different devices: /device:TPU:96 before, /device:TPU:165 now
where the time goes in v4:
time: 160 us
  Pallas kernels  136 us (85%)
  starting transfers between devices  12.3 us (8%)
  local copies, waits for them, and re-layouts  8.5 us (5%)
  other arithmetic  3.12 us (2%)
    pallas_call x1, Pallas kernels, ladder_of(): pl.pallas_call(ladder_kernel, out_shape=jax.ShapeDtypeStruct((2, n, n), F...  136 us
    ppermute x1, starting transfers between devices, shards(): received = lax.ppermute(other, ('pi', 'pj'), route(count_i, count_j))  12.3 us
    transpose x1, local copies, waits for them, and re-layouts, shards(): vectors = jnp.transpose(cholesky, (2, 0, 1)).reshape(-1, n)  6.74 us
  transfers between devices with their start and end apart: 1, of which 0 were waited for; matrix products, arithmetic and copies ran while one was open for 4% of the time, Pallas kernels for 0%

profile of v4, /device:TPU:165, one launch (start us, length us, event | category | flops | bytes accessed | tf_op | source)
XLA Modules:
  0.0 159.7 jit_solution(3765835141766593657)
XLA Ops:
  0.0 0.8 convert_element_type.7
  0.9 0.9 select_bitcast_fusion.1
  1.8 0.1 copy.5
  1.9 12.3 %collective-permute-start = (f32[2,128,128]{1,2,0:T(8,128)S(1)}, f32[2,128,128]{1,2,0:T(8,128)S(1)}, u32[]{:S(2)}, u32[]{:S(2)}) collective-permute-start(f32[2,128,128]{1,2,0:T(8,128)S(1)} %copy.5), channel_id=1, source_target_pairs={{0,1},{1,0},{2,33},{3,32},{4,65},{5,64},{6,97},{7,96},{8,129},{9,1... | collective-permute-start | bytes 393224 | tf_op jit(solution)/shard_map/ppermute | solution.py:379
  14.2 0.1 copy.6
  14.3 6.7 %copy.4 = bf16[128,128,128]{2,1,0:T(8,128)(2,1)} copy(bf16[128,128,128]{0,2,1:T(8,128)(2,1)} %bitcast.28) | data formatting | bytes 8388608 | tf_op jit(solution)/shard_map/transpose | solution.py:382
  21.1 0.0 collective-permute-done
  21.1 0.6 fusion.6.own
  21.7 0.7 fusion.3.base
  22.4 135.7 %shard_map.37 = f32[2,128,128]{2,1,0:T(8,128)} custom-call(bf16[16384,128]{1,0:T(8,128)(2,1)} %bitcast.27, bf16[2,128,128]{2,1,0:T(8,128)(2,1)} %fusion.6.own, f32[2,128,128]{2,1,0:T(8,128)} %fusion.3.base), custom_call_target="tpu_custom_call" | custom-call | tf_op jit(solution)/shard_map/pallas_call | solution.py:324
  158.1 1.6 copy.10
  (1 shorter events, 0.0 us)
Async XLA Ops:
  1.9 19.2 %collective-permute-start = (f32[2,128,128]{1,2,0:T(8,128)S(1)}, f32[2,128,128]{1,2,0:T(8,128)S(1)}, u32[]{:S(2)}, u32[]{:S(2)}) collective-permute-start(f32[2,128,128]{1,2,0:T(8,128)S(1)} %copy.5), channel_id=1, source_target_pairs={{0,1},{1,0},{2,33},{3,32},{4,65},{5,64},{6,97},{7,96},{8,129},{9,1... | collective-permute-start | bytes 393224 | tf_op jit(solution)/shard_map/ppermute | solution.py:379

commit v5 on v4

--- a/solution.py
+++ b/solution.py
@@ -27,9 +27,9 @@
 
 
 def ladder_kernel(
-    vec, own, base, out,
-    pairs, extra, work, acc, acc_own, acc_x, part, part_x, got_z, got_zx, total, send_y, got_y, send_yx, got_yx, done, got_m,
-    hs, hr, zs, zr, fs, fr, xs, xr, rs, rr, rxs, rxr, ss, sr, sxs, sxr, ms, mr,
+    vec, own, others, out,
+    pairs, extra, work, acc, acc_own, acc_x, part, part_x, got_z, got_zx, total, send_y, got_y, send_yx, got_yx, done, got_m, got_o, base,
+    hs, hr, zs, zr, fs, fr, xs, xr, rs, rr, rxs, rxr, ss, sr, sxs, sxr, ms, mr, os, orr,
 ):
     row = lax.axis_index("pi")
     col = lax.axis_index("pj")
@@ -182,6 +182,19 @@
     group((0,), beside=lambda: forward((1, 2, 3)))
     acc_own[...] = acc[0 : NY * n, :]
     forward((4, 5, 6, 7))
+    apart = (side, 2 * row + 1 - kept)
+    sibling = (row, 2 * row)
+
+    def o_copy(to):
+        return copy(others.at[1], got_o, os, orr, to)
+
+    @pl.when(off)
+    def _():
+        o_copy(apart).start()
+
+    @pl.when(is_y)
+    def _():
+        o_copy((row, col_x)).start()
 
     ready(2)
     ready(3)
@@ -235,6 +248,20 @@
     @pl.when(near_x)
     def _():
         sx_copy(gap_y).start()
+
+    @pl.when(off)
+    def _():
+        o_copy(apart).wait_recv()
+        base[...] = others[0] + got_o[...].T
+
+    @pl.when(jnp.logical_not(off))
+    def _():
+        base[...] = others[0] + others[0].T
+
+    @pl.when(is_x)
+    def _():
+        o_copy(sibling).wait_recv()
+        done[...] = others[1] + got_o[...].T
 
     ready(1)
     group((1,))
@@ -251,7 +278,6 @@
         return copy(done, got_m, ms, mr, to)
 
     mate = (side, 2 * row + kept)
-    sibling = (row, 2 * row)
 
     @pl.when(is_x)
     def _():
@@ -260,7 +286,7 @@
         for k in range(1, NY):
             copy(send_yx, got_yx.at[k], sxs, sxr.at[k], at(z, ahead(k))).wait_recv()
             whole = whole + got_yx[k].astype(F32)
-        done[...] = base[1] + 0.5 * whole
+        done[...] += 0.5 * whole
         m_copy(sibling).start()
         out[0] = done[...]
 
@@ -268,7 +294,7 @@
     for k in range(1, NY):
         s_copy(k).wait_recv()
         ladder = ladder + got_y[k].astype(F32)
-    finished = base[0] + 0.5 * ladder
+    finished = base[...] + 0.5 * ladder
     out[kept] = finished
 
     @pl.when(off)
@@ -301,6 +327,14 @@
     def _():
         sx_copy(gap_y).wait_send()
 
+    @pl.when(off)
+    def _():
+        o_copy(apart).wait_send()
+
+    @pl.when(is_y)
+    def _():
+        o_copy((row, col_x)).wait_send()
+
     @pl.when(is_x)
     def _():
         m_copy(sibling).wait_send()
@@ -316,7 +350,7 @@
         out[1] = got_m[...].T
 
 
-def ladder_of(vectors, own, base):
+def ladder_of(vectors, own, others):
     n = own.shape[-1]
     dma = pltpu.SemaphoreType.DMA
     vmem = pltpu.VMEM
@@ -344,6 +378,8 @@
             vmem((NY, n, n), BF16),
             vmem((n, n), F32),
             vmem((n, n), F32),
+            vmem((n, n), F32),
+            vmem((n, n), F32),
             dma((NY,)), dma((NY,)),
             dma((NZ,)), dma((NZ,)),
             dma((NY * NZ,)), dma((NY * NZ,)),
@@ -353,11 +389,12 @@
             dma((NY,)), dma((NY,)),
             dma, dma((NY,)),
             dma, dma,
+            dma, dma,
         ],
         compiler_params=pltpu.CompilerParams(
             collective_id=0, has_side_effects=True, vmem_limit_bytes=56 * 2**20
         ),
-    )(vectors, own, base)
+    )(vectors, own, others)
 
 
 def shards(amplitudes, cholesky, other_terms):
@@ -373,14 +410,20 @@
     def pick(pair, which):
         return jnp.where(which, pair[1], pair[0])
 
-    a = amplitudes[:, 0].astype(F32)
-    both = jnp.stack([a, other_terms[:, 0]], axis=1)
-    kept, other = pick(both, second), pick(both, ~second)
+    a = amplitudes[:, 0]
+    o = other_terms[:, 0]
+    kept, other = pick(a, second), pick(a, ~second)
     received = lax.ppermute(other, ("pi", "pj"), route(count_i, count_j))
     mate = jnp.where(diagonal, kept, received)
-    sums = jnp.stack([kept + mate.swapaxes(1, 2), other + received.swapaxes(1, 2)])
+    own = jnp.stack(
+        [
+            kept.astype(F32) + mate.astype(F32).T,
+            other.astype(F32) + received.astype(F32).T,
+        ]
+    ).astype(BF16)
+    others = jnp.stack([pick(o, second), pick(o, ~second)])
     vectors = jnp.transpose(cholesky, (2, 0, 1)).reshape(-1, n)
-    return ladder_of(vectors, sums[:, 0].astype(BF16), sums[:, 1])[:, None]
+    return ladder_of(vectors, own, others)[:, None]
 
 
 def solution(mesh):

time: 160 us -> 157 us (0.981)
  the two profiles are of different devices: /device:TPU:165 before, /device:TPU:35 now
where the time goes in v5:
time: 157 us
  Pallas kernels  128 us (82%)
  starting transfers between devices  17.3 us (11%)
  local copies, waits for them, and re-layouts  9.18 us (6%)
  other arithmetic  2.37 us (2%)
    pallas_call x1, Pallas kernels, ladder_of(): pl.pallas_call(ladder_kernel, out_shape=jax.ShapeDtypeStruct((2, n, n), F...  128 us
    ppermute x1, starting transfers between devices, shards(): received = lax.ppermute(other, ('pi', 'pj'), route(count_i, count_j))  17.3 us
    transpose x1, local copies, waits for them, and re-layouts, shards(): vectors = jnp.transpose(cholesky, (2, 0, 1)).reshape(-1, n)  6.67 us
  transfers between devices with their start and end apart: 1, of which 0 were waited for; matrix products, arithmetic and copies ran while one was open for 5% of the time, Pallas kernels for 0%

profile of v5, /device:TPU:35, one launch (start us, length us, event | category | flops | bytes accessed | tf_op | source)
XLA Modules:
  0.0 156.6 jit_solution(6419800596823326967)
XLA Ops:
  0.0 0.8 select_bitcast_fusion.3
  0.8 17.3 %collective-permute-start = (bf16[128,128]{1,0:T(8,128)(2,1)S(1)}, bf16[128,128]{1,0:T(8,128)(2,1)S(1)}, u32[]{:S(2)}, u32[]{:S(2)}) collective-permute-start(bf16[128,128]{1,0:T(8,128)(2,1)S(1)} %get-tuple-element.8), channel_id=1, source_target_pairs={{0,1},{1,0},{2,33},{3,32},{4,65},{5,64},{6,97},{7,96},{8,129},{9,1... | collective-permute-start | bytes 98312 | tf_op jit(solution)/shard_map/ppermute | solution.py:416
  18.0 0.9 select_bitcast_fusion.1
  18.9 0.7 pad_maximum_fusion.others
  19.6 0.1 copy.6
  19.7 0.1 copy.5
  19.8 6.7 %copy.4 = bf16[128,128,128]{2,1,0:T(8,128)(2,1)} copy(bf16[128,128,128]{0,2,1:T(8,128)(2,1)} %bitcast.30) | data formatting | bytes 8388608 | tf_op jit(solution)/shard_map/transpose | solution.py:425
  26.5 0.0 collective-permute-done
  26.5 0.7 copy.7.own
  27.3 127.7 %shard_map.37 = f32[2,128,128]{2,1,0:T(8,128)} custom-call(bf16[16384,128]{1,0:T(8,128)(2,1)} %bitcast.29, bf16[2,128,128]{2,1,0:T(8,128)(2,1)} %copy.7.own, f32[2,128,128]{2,1,0:T(8,128)} %pad_maximum_fusion.others), custom_call_target="tpu_custom_call" | custom-call | tf_op jit(solution)/shard_map/pallas_call | solution.py:358
  155.0 1.6 %copy.10 = f32[2,1,128,128]{3,2,1,0:T(8,128)} copy(f32[2,1,128,128]{3,2,1,0:T(8,128)} %bitcast.31) | data formatting | bytes 262144
  (2 shorter events, 0.0 us)
Async XLA Ops:
  0.8 25.7 %collective-permute-start = (bf16[128,128]{1,0:T(8,128)(2,1)S(1)}, bf16[128,128]{1,0:T(8,128)(2,1)S(1)}, u32[]{:S(2)}, u32[]{:S(2)}) collective-permute-start(bf16[128,128]{1,0:T(8,128)(2,1)S(1)} %get-tuple-element.8), channel_id=1, source_target_pairs={{0,1},{1,0},{2,33},{3,32},{4,65},{5,64},{6,97},{7,96},{8,129},{9,1... | collective-permute-start | bytes 98312 | tf_op jit(solution)/shard_map/ppermute | solution.py:416
